TPU v7x, 256 devices: a whole 4x4x8 slice. The times are simulated.
256 devices in a mesh: energy: 8 (over z), atom: 32 (over x, y, core).
Axes of the slice: x: 4, y: 4, z: 8, core: 2. Of those that a mesh axis runs over, the one named last changes fastest.
Arguments:
- t_mats: bfloat16 [8, 64, 2048], P('energy', 'atom'), may hold values from -0.75 to 0.75
- struct_table: bfloat16 [8, 64, 2048], P('energy'), may hold values from -0.359375 to 0.359375
- zone_atoms: int32 [64, 64], P('atom'), may hold values from 0 to 63, as said below
- zone_size: int32 [64], P('atom'), may hold values from 32 to 64
- pair_index: int32 [64, 384], P('atom'), may hold values from 0 to 63
- zone_link: int32 [64, 384], P('atom'), may hold values from 0 to 63
- weights: float32 [8, 2], P('energy'), may hold values from -1 to 1
Outputs:
- green: float32 [64, 2048], P('atom')
Inputs may be any that keep to these rules, and one draw needn't show every extreme that they name: Atom g is owned by index g // 2 of the atom axis; zone_atoms[g, 0] is g; the owner of every member of atom g's zone lies -16 to 15 steps from g's owner along the atom axis, counted around the axis, and both extreme offsets occur in every zone; members may repeat (periodic images).
All inputs are finite; a program needn't handle non-finite values.
Results may differ from a plain program's by a relative error of at most 0.003.
Values may be sent and summed in bfloat16 or wider, within the bound.
A program may use at most 128 MiB of HBM per device.

v0:
```python
import jax
import jax.numpy as jnp
from jax import lax
from jax.sharding import PartitionSpec as P

L = 32
Z = 64
NB = 6
ITERS = 3


def real_form(block):
    parts = block.reshape(block.shape[:-1] + (2, L, L))
    real_part = parts[..., 0, :, :]
    imag_part = parts[..., 1, :, :]
    top_rows = jnp.concatenate([real_part, -imag_part], axis=-1)
    bottom_rows = jnp.concatenate([imag_part, real_part], axis=-1)
    return jnp.concatenate([top_rows, bottom_rows], axis=-2)


def scatter_terms(couplings, gathered, pattern):
    products = jnp.einsum(pattern, couplings, gathered, preferred_element_type=jnp.float32)
    real_part = products[..., 0, 0, :, :] - products[..., 1, 1, :, :]
    imag_part = products[..., 1, 0, :, :] + products[..., 0, 1, :, :]
    return jnp.concatenate([real_part, imag_part], axis=-2)


def take_links(column_parts, link_rows):
    return jax.vmap(
        lambda member_col, member_links: member_col[:, member_links], in_axes=(1, 0), out_axes=1
    )(column_parts, link_rows)


def solve_zones(zone_block, couplings_flat, links):
    e_dev, a_dev = (zone_block.shape[0], zone_block.shape[1])
    t_real = real_form(zone_block)
    couplings = couplings_flat.reshape(e_dev, a_dev, Z, NB, 2, L, L)
    start_block = t_real[:, :, 0, :, :L].astype(jnp.float32)
    start = jnp.zeros((e_dev, a_dev, Z, 2 * L, L), jnp.float32).at[:, :, 0].set(start_block)
    column = start
    for repeat in range(ITERS - 1):
        column_parts = column.astype(jnp.bfloat16).reshape(e_dev, a_dev, Z, 2, L, L)
        gathered = take_links(column_parts, links).reshape(e_dev, a_dev, Z, NB, 2, L, L)
        coupled = scatter_terms(couplings, gathered, "eganpij,eganqjk->egapqik").astype(
            jnp.bfloat16
        )
        column = (
            jnp.einsum("egaij,egajk->egaik", t_real, coupled, preferred_element_type=jnp.float32)
            + start
        )
    column_parts = column.astype(jnp.bfloat16).reshape(e_dev, a_dev, Z, 2, L, L)
    gathered = take_links(column_parts, links[:, :NB])
    coupled = scatter_terms(couplings[:, :, 0], gathered, "egnpij,egnqjk->egpqik").astype(
        jnp.bfloat16
    )
    return (
        jnp.einsum("egij,egjk->egik", t_real[:, :, 0], coupled, preferred_element_type=jnp.float32)
        + start_block
    )


def body(t_mats, struct_table, zone_atoms, zone_size, pair_index, zone_link, weights):
    e_dev, a_dev, block_flat = t_mats.shape
    window = lax.all_gather(t_mats, "atom", axis=1, tiled=True)
    present = jnp.arange(Z, dtype=jnp.int32)[None, :] < zone_size[:, None]
    zone_block = jnp.where(
        present[None, :, :, None], window[:, zone_atoms], jnp.zeros((), jnp.bfloat16)
    )
    couplings_flat = struct_table[:, pair_index]
    diagonal = solve_zones(zone_block, couplings_flat, zone_link)
    real_rows = diagonal[:, :, :L, :].reshape(e_dev, a_dev, L * L)
    imag_rows = diagonal[:, :, L:, :].reshape(e_dev, a_dev, L * L)
    w_real = weights[:, 0][:, None, None]
    w_imag = weights[:, 1][:, None, None]
    green_real = jnp.sum(w_real * real_rows - w_imag * imag_rows, axis=0)
    green_imag = jnp.sum(w_real * imag_rows + w_imag * real_rows, axis=0)
    local_green = jnp.concatenate([green_real, green_imag], axis=-1)
    return lax.psum(local_green, "energy")


def solution(mesh):
    return jax.shard_map(
        body,
        mesh=mesh,
        in_specs=(
            P("energy", "atom", None),
            P("energy", None, None),
            P("atom", None),
            P("atom"),
            P("atom", None),
            P("atom", None),
            P("energy", None),
        ),
        out_specs=P("atom", None),
        check_vma=False,
    )
```

profile of v0, /device:TPU:2, one launch (start us, length us, event | category | flops | bytes accessed | tf_op | source)
XLA Modules:
  0.0 181.2 jit_solution(2363927497091238241)
XLA Ops:
  0.0 0.8 copy.91
  0.8 24.8 %all_gather.3 = bf16[1,64,2048]{2,0,1:T(2,128)(2,1)S(1)} all-gather(bf16[1,2,2048]{2,0,1:T(2,128)(2,1)S(1)} %copy.91), channel_id=1, replica_groups=mesh['energy'=8,'atom'=32] {'atom'}, dimensions={1}, use_global_device_ids=true | all-gather | bytes 270336 | tf_op jit(solution)/shard_map/all_gather | solution.py:64
  25.6 0.2 copy.168
  25.7 0.7 compare_select_fusion.3
  26.4 0.1 reshape.287
  26.5 0.9 gather_fusion
  27.4 0.3 copy.92
  27.7 0.4 gather.18
  28.1 2.1 %copy.93 = bf16[1,2,64,2,32,32]{5,4,2,1,3,0:T(8,128)(2,1)S(1)} copy(bf16[1,2,64,2,32,32]{2,1,5,4,3,0:T(2,128)(2,1)S(1)} %gather.18) | data formatting | bytes 1048576 | tf_op jit(solution)/shard_map/gather | solution.py:67
  30.3 0.1 iota_compare_fusion
  30.4 0.2 broadcast_select_fusion
  30.6 0.4 slice_bitcast_fusion.4
  31.0 0.1 fusion.57
  31.1 1.2 maximum_maximum_fusion
  32.3 0.5 scatter.9
  32.9 0.8 copy-done.4
  33.7 9.2 %gather_fusion.2 = bf16[768,2,32,32]{3,2,1,0:T(8,128)(2,1)} fusion(bf16[2,64,2,32,32]{4,3,2,1,0:T(8,128)(2,1)S(1)} %bitcast.152, s32[768]{0:T(1024)S(1)} %reshape.305), kind=kCustom, calls=%fused_computation.2 | custom fusion | bytes 6297600 | tf_op jit(solution)/shard_map/vmap()/gather | solution.py:30
  42.9 3.4 %gather_fusion.1 = bf16[768,2048]{1,0:T(8,128)(2,1)S(1)} fusion(bf16[64,2048]{1,0:T(8,128)(2,1)S(1)} %bitcast.151, s32[1024]{0:T(1024)S(1)} %pad_clamp_fusion), kind=kCustom, calls=%fused_computation.1 | custom fusion | bytes 6294528 | tf_op jit(solution)/shard_map/gather | solution.py:69
  46.4 11.8 %reshape.277 = bf16[2,64,6,2,32,32]{5,4,3,2,1,0:T(8,128)(2,1)} reshape(bf16[768,2048]{1,0:T(8,128)(2,1)S(1)} %gather_fusion.1) | data formatting | bytes 6291456 | tf_op jit(solution)/shard_map/reshape.48
  58.2 17.2 %fusion.6 = f32[1,2,64,2,2,32,32]{5,6,3,4,2,1,0:T(8,128)} fusion(bf16[2,64,6,2,32,32,1]{5,4,3,2,1,0,6:T(8,128)(2,1)} %bitcast.155, bf16[2,64,6,2,32,32]{5,4,3,2,1,0:T(8,128)(2,1)} %reshape.277), kind=kOutput, calls=%fused_computation.11 | convolution fusion | flops 201326592 | bytes 8388608 | tf_op jit(solution)/shard_map/eganpij,eganqjk->egapqik/dot_general | solution.py:22
  75.3 2.7 %fusion.27 = bf16[2,64,32,32]{2,3,1,0:T(8,128)(2,1)S(1)} fusion(f32[1,2,64,2,2,32,32]{5,6,3,4,2,1,0:T(8,128)} %fusion.6), kind=kLoop, calls=%fused_computation.34 | loop fusion | flops 262144 | bytes 1310720 | tf_op jit(solution)/shard_map/sub | solution.py:23
  78.1 2.9 %fusion.28 = bf16[2,64,32,32]{2,3,1,0:T(8,128)(2,1)S(1)} fusion(f32[1,2,64,2,2,32,32]{5,6,3,4,2,1,0:T(8,128)} %fusion.6), kind=kLoop, calls=%fused_computation.35 | loop fusion | flops 262144 | bytes 1310720 | tf_op jit(solution)/shard_map/add | solution.py:24
  81.0 1.3 fusion.24
  82.3 1.3 copy-done.7
  83.6 0.1 copy.140
  83.8 0.6 constant_dynamic-update-slice_fusion.1
  84.4 1.8 %convert_element_type.37 = bf16[1,2,64,64,32]{3,4,2,1,0:T(8,128)(2,1)S(1)} convert(f32[1,2,64,64,32]{3,4,2,1,0:T(8,128)} %constant_dynamic-update-slice_fusion.1) | non-fusion elementwise | flops 262144 | bytes 1572864 | tf_op jit(solution)/shard_map/convert_element_type | solution.py:42
  86.2 1.2 copy.129
  87.4 9.4 %gather_fusion.3 = bf16[768,2,32,32]{3,2,1,0:T(8,128)(2,1)} fusion(bf16[2,64,2,32,32]{4,3,2,1,0:T(8,128)(2,1)S(1)} %bitcast.153, s32[768]{0:T(1024)S(1)} %reshape.305), kind=kCustom, calls=%fused_computation.3 | custom fusion | bytes 6297600 | tf_op jit(solution)/shard_map/vmap()/gather | solution.py:30
  96.8 17.2 %fusion.11 = f32[1,2,64,2,2,32,32]{5,6,3,4,2,1,0:T(8,128)} fusion(bf16[2,64,6,2,32,32,1]{5,4,3,2,1,0,6:T(8,128)(2,1)} %bitcast.156, bf16[2,64,6,2,32,32]{5,4,3,2,1,0:T(8,128)(2,1)} %reshape.277), kind=kOutput, calls=%fused_computation.12 | convolution fusion | flops 201326592 | bytes 8388608 | tf_op jit(solution)/shard_map/eganpij,eganqjk->egapqik/dot_general | solution.py:22
  114.0 2.7 %fusion.29 = bf16[2,64,32,32]{2,3,1,0:T(8,128)(2,1)S(1)} fusion(f32[1,2,64,2,2,32,32]{5,6,3,4,2,1,0:T(8,128)} %fusion.11), kind=kLoop, calls=%fused_computation.36 | loop fusion | flops 262144 | bytes 1310720 | tf_op jit(solution)/shard_map/sub | solution.py:23
  116.8 2.9 %fusion.30 = bf16[2,64,32,32]{2,3,1,0:T(8,128)(2,1)S(1)} fusion(f32[1,2,64,2,2,32,32]{5,6,3,4,2,1,0:T(8,128)} %fusion.11), kind=kLoop, calls=%fused_computation.37 | loop fusion | flops 262144 | bytes 1310720 | tf_op jit(solution)/shard_map/add | solution.py:24
  119.7 1.3 fusion.22
  120.9 1.3 copy-done.8
  122.3 0.1 copy.143
  122.4 0.6 constant_dynamic-update-slice_fusion
  123.1 2.8 %convert_element_type.38 = bf16[1,2,64,64,32]{3,4,2,1,0:T(8,128)(2,1)} convert(f32[1,2,64,64,32]{3,4,2,1,0:T(8,128)} %constant_dynamic-update-slice_fusion) | non-fusion elementwise | flops 262144 | bytes 1572864 | tf_op jit(solution)/shard_map/convert_element_type | solution.py:51
  125.9 2.9 %copy.134 = bf16[1,2,64,64,32]{4,3,2,1,0:T(8,128)(2,1)} copy(bf16[1,2,64,64,32]{3,4,2,1,0:T(8,128)(2,1)} %convert_element_type.38) | data formatting | bytes 1048576 | tf_op jit(solution)/shard_map/vmap()/transpose;reshape | solution.py:30
  128.8 0.1 reshape.321
  128.9 2.9 %gather_fusion.4 = bf16[12,2,32,32]{3,2,1,0:T(8,128)(2,1)} fusion(bf16[2,64,2,32,32]{4,3,2,1,0:T(8,128)(2,1)} %bitcast.159, s32[12]{0:T(128)S(1)} %reshape.321), kind=kCustom, calls=%fused_computation.4 | custom fusion | bytes 98400 | tf_op jit(solution)/shard_map/vmap()/gather | solution.py:30
  131.8 11.6 %reshape.280 = bf16[1,2,64,6,2,32,32]{6,5,4,3,2,1,0:T(8,128)(2,1)} reshape(bf16[768,2048]{1,0:T(8,128)(2,1)S(1)} %copy-done.3) | data formatting | bytes 6291456 | tf_op jit(solution)/shard_map/reshape | solution.py:37
  143.4 1.3 convolution_bitcast_fusion
  144.8 1.0 fusion.26
  145.8 0.6 fusion.58
  146.4 1.2 multiply_subtract_fusion
  147.7 0.1 add.92
  147.7 0.1 sub.43
  147.8 33.3 %psum.7 = f32[2,2048]{1,0:T(2,128)} all-reduce(f32[2,2048]{1,0:T(2,128)S(1)} %pad_maximum_fusion), channel_id=1, replica_groups=mesh['energy'=8,'atom'=32] {'energy'}, use_global_device_ids=true, to_apply=%region_0.1 | all-reduce | flops 4096 | bytes 32768 | tf_op jit(solution)/shard_map/psum | solution.py:78
  (40 shorter events, 0.3 us)
Async XLA Ops:
  0.0 42.9 %copy-start = (bf16[1,64,2048]{2,1,0:T(8,128)(2,1)S(1)}, bf16[1,64,2048]{2,1,0:T(8,128)(2,1)}, u32[]{:S(2)}) copy-start(bf16[1,64,2048]{2,1,0:T(8,128)(2,1)} %param.10) | copy-start | bytes 786436
  27.7 2.6 %copy-start.12 = (s32[2]{0:T(128)S(1)}, s32[2]{0:T(128)}, u32[]{:S(2)}) copy-start(s32[2]{0:T(128)} %param.12) | copy-start | bytes 28
  32.3 1.4 copy-start.4
  32.3 1.4 copy-start.9
  33.7 9.2 %copy-start.10 = (s32[2,384]{1,0:T(2,128)S(1)}, s32[2,384]{1,0:T(2,128)}, u32[]{:S(2)}) copy-start(s32[2,384]{1,0:T(2,128)} %param.13) | copy-start | bytes 9220
  46.3 11.8 %copy-start.2 = (bf16[768,2048]{1,0:T(8,128)(2,1)}, bf16[768,2048]{1,0:T(8,128)(2,1)S(1)}, u32[]{:S(2)}) copy-start(bf16[768,2048]{1,0:T(8,128)(2,1)S(1)} %gather_fusion.1) | copy-start | bytes 9437188
  78.1 2.9 %copy-start.5 = (bf16[1,2,64,64,64]{4,3,2,1,0:T(8,128)(2,1)S(1)}, bf16[1,2,64,64,64]{4,3,2,1,0:T(8,128)(2,1)}, u32[]{:S(2)}) copy-start(bf16[1,2,64,64,64]{4,3,2,1,0:T(8,128)(2,1)} %copy-done.4) | copy-start | bytes 3145732
  82.3 1.3 copy-start.7
  116.7 2.9 %copy-start.6 = (bf16[1,2,64,64,64]{4,3,2,1,0:T(8,128)(2,1)S(1)}, bf16[1,2,64,64,64]{4,3,2,1,0:T(8,128)(2,1)}, u32[]{:S(2)}) copy-start(bf16[1,2,64,64,64]{4,3,2,1,0:T(8,128)(2,1)} %copy-done.4) | copy-start | bytes 3145732
  120.9 1.3 copy-start.8
  125.9 5.9 %copy-start.3 = (bf16[768,2048]{1,0:T(8,128)(2,1)S(1)}, bf16[768,2048]{1,0:T(8,128)(2,1)}, u32[]{:S(2)}) copy-start(bf16[768,2048]{1,0:T(8,128)(2,1)} %copy-done.2) | copy-start | bytes 9437188
  131.8 14.0 %copy-start.11 = (f32[1,2]{1,0:T(1,128)S(1)}, f32[1,2]{1,0:T(1,128)}, u32[]{:S(2)}) copy-start(f32[1,2]{1,0:T(1,128)} %param.15) | copy-start | bytes 28
  131.8 49.4 %copy-start.1 = (bf16[1,64,2048]{2,1,0:T(8,128)(2,1)S(1)}, bf16[1,64,2048]{2,1,0:T(8,128)(2,1)}, u32[]{:S(2)}) copy-start(bf16[1,64,2048]{2,1,0:T(8,128)(2,1)} %param.10) | copy-start | bytes 786436
where the time goes:
time: 182 us; the launch traced here: 181 us
  local copies, waits for them, and re-layouts  64 us (35%)
  blocking collectives  58.1 us (32%)
  matrix products  39.3 us (22%)
  other arithmetic  19.4 us (11%)
    dot_general x3, matrix products, scatter_terms(): jnp.einsum(pattern, couplings, gathered, preferred_element_type=jnp.float32)  35.7 us
    psum x1, blocking collectives, body(): return lax.psum(local_green, 'energy')  33.3 us
    all_gather x1, blocking collectives, body(): window = lax.all_gather(t_mats, 'atom', axis=1, tiled=True)  24.8 us
    gather x5, local copies, waits for them, and re-layouts, take_links(): member_col[:, member_links]  21.6 us
    another operation x3, local copies, waits for them, and re-layouts  11.8 us
    reshape x1, local copies, waits for them, and re-layouts, solve_zones(): couplings = couplings_flat.reshape(e_dev, a_dev, Z, NB, 2, L, L)  11.6 us
    add x3, other arithmetic, scatter_terms(): imag_part = products[..., 1, 0, :, :] + products[..., 0, 1, :, :]  5.8 us
    sub x3, other arithmetic, scatter_terms(): real_part = products[..., 0, 0, :, :] - products[..., 1, 1, :, :]  5.49 us

commit v1 on v0

v1 whole, which is shorter than its diff:
```python
import functools

import jax
import jax.numpy as jnp
from jax import lax
from jax.experimental import pallas as pl
from jax.experimental.pallas import tpu as pltpu
from jax.sharding import PartitionSpec as P

L = 32
Z = 64
NB = 6
KTAB = 64
ROWS = 16
LANES = 128
FORM = 64
MESH = pl.DeviceIdType.MESH
NT = (((1,), (1,)), ((), ()))


def iota2(shape, dim):
    return lax.broadcasted_iota(jnp.int32, shape, dim)


def dot_nt(a, b):
    return lax.dot_general(a, b, NT, preferred_element_type=jnp.float32)


def dot(a, b):
    return jnp.dot(a, b, preferred_element_type=jnp.float32)


def to_bf16_mask(cond):
    return jnp.where(cond, 1.0, 0.0).astype(jnp.bfloat16)


def form_matrix():
    i = iota2((256, 512), 0)
    j = iota2((256, 512), 1)
    h, s1, c = i >> 7, (i >> 5) & 3, i & 31
    s, l = j >> 7, j & 127
    return to_bf16_mask(
        (s1 == s) & (l < 64) & (((l >> 3) & 1) == h) & (((l & 7) * 4 + (l >> 4)) == c)
    )


def spread_matrix():
    i = iota2((64, 256), 0)
    j = iota2((64, 256), 1)
    return to_bf16_mask(
        (((i >> 3) & 1) == (j >> 7)) & (((i & 7) * 4 + (i >> 4)) == (j & 31))
    )


def start_matrix():
    k = iota2((L, FORM), 0)
    l = iota2((L, FORM), 1)
    return to_bf16_mask((((l >> 3) & 1) == 0) & (((l & 7) * 4 + (l >> 4)) == k))


def partner(x):
    n = x.shape[0] // ROWS
    halves = x.reshape(n, 2, 8, LANES)
    return jnp.concatenate([-halves[:, 1:], halves[:, :1]], axis=1).reshape(n * ROWS, LANES)


def with_partner(x32):
    return jnp.concatenate(
        [x32.astype(jnp.bfloat16), partner(x32).astype(jnp.bfloat16)], axis=1
    )


def kernel(
    ne, na, adev,
    t_hbm, tab_hbm, atoms_hbm, size_hbm, pair_hbm, link_hbm, w_hbm,
    out_ref,
    t_ref, tab_ref, atoms, size, pair, link, w_ref,
    xf, gath, tabx, gform, tform, pbuf, c1, c1rep, near, arbuf,
    in_sems, ag_send, ag_recv, ar_send, ar_recv,
):
    e = lax.axis_index("energy")
    me = lax.axis_index("atom")
    n_atoms = na * adev
    blk = adev * ROWS

    sources = (t_hbm, tab_hbm, link_hbm, pair_hbm, atoms_hbm, size_hbm, w_hbm)
    landed = (t_ref, tab_ref, link, pair, atoms, size, w_ref)
    loads = [
        pltpu.make_async_copy(src, dst, in_sems.at[i])
        for i, (src, dst) in enumerate(zip(sources, landed))
    ]
    for copy in loads:
        copy.start()

    barrier = pltpu.get_barrier_semaphore()

    def greet_atom(d, _):
        pl.semaphore_signal(
            barrier, inc=1, device_id=(e, lax.rem(me + d, na)), device_id_type=MESH
        )
        return 0

    def greet_energy(d, _):
        pl.semaphore_signal(
            barrier, inc=1, device_id=(lax.rem(e + d, ne), me), device_id_type=MESH
        )
        return 0

    lax.fori_loop(1, na, greet_atom, 0)
    lax.fori_loop(1, ne, greet_energy, 0)

    loads[0].wait()
    for t in range(ROWS):
        xf[pl.ds(t, adev, stride=ROWS), :] = t_ref[
            0, :, t * LANES : (t + 1) * LANES
        ].astype(jnp.float32)
    own32 = xf[...]
    own = own32.astype(jnp.bfloat16)
    my_rows = pl.ds(me * adev, adev)
    for z in range(adev):
        gath[me * adev + z] = own[z * ROWS : (z + 1) * ROWS]
    gath[n_atoms] = jnp.zeros((ROWS, LANES), jnp.bfloat16)

    pl.semaphore_wait(barrier, na - 1 + ne - 1)

    def send(d, _):
        pltpu.make_async_remote_copy(
            src_ref=gath.at[my_rows],
            dst_ref=gath.at[my_rows],
            send_sem=ag_send,
            recv_sem=ag_recv,
            device_id=(e, lax.rem(me + d, na)),
            device_id_type=MESH,
        ).start()
        return 0

    lax.fori_loop(1, na, send, 0)

    ab = form_matrix()
    loads[1].wait()
    for t in range(ROWS):
        tabx[pl.ds(t, KTAB, stride=ROWS), :] = tab_ref[
            0, :, t * LANES : (t + 1) * LANES
        ].astype(jnp.float32)

    def put_forms(dst, first, lhs):
        forms = dot(lhs, ab).astype(jnp.bfloat16)
        for k in range(lhs.shape[0] // ROWS):
            for s in range(4):
                dst[first + k, s * ROWS : (s + 1) * ROWS, :] = forms[
                    k * ROWS : (k + 1) * ROWS, s * LANES : (s + 1) * LANES
                ]

    def table_forms(i, _):
        rows = tabx[pl.ds(pl.multiple_of(i * 128, 128), 128), :]
        put_forms(gform, i * 8, with_partner(rows))
        return 0

    lax.fori_loop(0, KTAB // 8, table_forms, 0)
    put_forms(tform, 0, with_partner(own32))

    def form(ref, k):
        return ref[k][:, :FORM]

    sel = start_matrix()
    start = [dot_nt(sel, form(tform, z)) for z in range(adev)]
    start_all = jnp.concatenate(start, axis=0).astype(jnp.bfloat16)

    def table_times_start(i, _):
        for k in range(8):
            b = i * 8 + k
            term = dot_nt(start_all, form(gform, b))
            for z in range(adev):
                pbuf[z, b] = term[z * L : (z + 1) * L]
        return 0

    lax.fori_loop(0, KTAB // 8, table_times_start, 0)
    for z in range(adev):
        pbuf[z, KTAB] = jnp.zeros((L, FORM), jnp.float32)

    slots = NB * NB
    for copy in loads[2:]:
        copy.wait()
    for z in range(adev):

        def first_coupled(n, _, z=z):
            b = link[z, n]
            for m in range(NB):
                a = link[z, b * NB + m]
                acc = None
                for j in range(NB):
                    at = a * NB + j
                    term = pbuf[z, jnp.minimum(pair[z, at] + link[z, at] * KTAB, KTAB)]
                    acc = term if acc is None else acc + term
                c1[pl.ds(pl.multiple_of((z * slots + n * NB + m) * L, L), L), :] = acc.astype(
                    jnp.bfloat16
                )
            return 0

        lax.fori_loop(0, NB, first_coupled, 0)

    rep = spread_matrix()

    def spread(i, _):
        rows = pl.ds(pl.multiple_of(i * 256, 256), 256)
        c1rep[rows, :] = dot(c1[rows, :], rep).astype(jnp.bfloat16)
        return 0

    lax.fori_loop(0, adev * slots * L // 256, spread, 0)

    others = gath.at[pl.ds(0, (na - 1) * adev)]
    pltpu.make_async_copy(others, others, ag_recv).wait()
    pltpu.make_async_copy(others, others, ag_send).wait()

    lane_group = iota2((ROWS, LANES), 1) >> 5

    def member(z, a):
        absent = jnp.maximum(a - size[z] + 1, 0)
        return jnp.minimum(atoms[z, a] + absent * n_atoms, n_atoms)

    def is_first(a):
        return 1.0 - jnp.minimum(a, 1).astype(jnp.float32)

    def packed(atom):
        return gath[atom]

    def wide_form(x):
        x32 = x.astype(jnp.float32)
        y32 = jnp.concatenate([-x32[8:], x32[:8]], axis=0)

        def groups(v):
            return jnp.concatenate(
                [jnp.where(lane_group == s, v, 0.0).astype(jnp.bfloat16) for s in range(4)],
                axis=0,
            )

        return jnp.concatenate([groups(x32), groups(y32)], axis=1)

    for z in range(adev):
        x32 = jnp.concatenate(
            [packed(member(z, link[z, n])) for n in range(NB)], axis=0
        ).astype(jnp.float32)
        put_forms(tform, adev + z * NB, with_partner(x32))

    for z in range(adev):

        def first_column(n, _, z=z):
            b = link[z, n]
            for m in range(NB):
                a = link[z, b * NB + m]
                at = pl.ds(pl.multiple_of((z * slots + n * NB + m) * L, L), L)
                col = dot_nt(c1rep[at, :], wide_form(packed(member(z, a))))
                col = col + is_first(a) * start[z]
                near[at, :] = col.astype(jnp.bfloat16)
            return 0

        lax.fori_loop(0, NB, first_column, 0)

    lane_group_f = iota2((ROWS, LANES), 1) >> 5
    w_re = w_ref[0, 0]
    w_im = w_ref[0, 1]
    mine = pl.multiple_of(e * blk, blk)
    for z in range(adev):
        total = None
        for n in range(NB):
            b = link[z, n]
            acc = None
            for m in range(NB):
                at = (z * slots + n * NB + m) * L
                term = dot_nt(near[at : at + L, :], form(gform, pair[z, b * NB + m]))
                acc = term if acc is None else acc + term
            col = dot_nt(acc.astype(jnp.bfloat16), form(tform, adev + z * NB + n))
            col = col + is_first(b) * start[z]
            term = dot_nt(col.astype(jnp.bfloat16), form(gform, pair[z, n]))
            total = term if total is None else total + term
        coupled = total.astype(jnp.bfloat16)
        diag = dot_nt(form(tform, z), jnp.concatenate([coupled] * 4, axis=0))
        block = xf[z * ROWS : (z + 1) * ROWS, :]
        for s in range(4):
            block = block + jnp.where(
                lane_group_f == s, diag[s * ROWS : (s + 1) * ROWS, :], 0.0
            )
        re, im = block[:8], block[8:]
        arbuf[pl.ds(mine + z * ROWS, 8), :] = w_re * re - w_im * im
        arbuf[pl.ds(mine + z * ROWS + 8, 8), :] = w_re * im + w_im * re

    def share(d, _):
        pltpu.make_async_remote_copy(
            src_ref=arbuf.at[pl.ds(mine, blk)],
            dst_ref=arbuf.at[pl.ds(mine, blk)],
            send_sem=ar_send,
            recv_sem=ar_recv,
            device_id=(lax.rem(e + d, ne), me),
            device_id_type=MESH,
        ).start()
        return 0

    lax.fori_loop(1, ne, share, 0)
    rest = arbuf.at[pl.ds(0, (ne - 1) * blk)]
    pltpu.make_async_copy(rest, rest, ar_recv).wait()
    pltpu.make_async_copy(rest, rest, ar_send).wait()
    green = arbuf[0:blk, :]
    for i in range(1, ne):
        green = green + arbuf[i * blk : (i + 1) * blk, :]
    out_ref[...] = green


def body(t_mats, struct_table, zone_atoms, zone_size, pair_index, zone_link, weights, ne, na):
    adev = t_mats.shape[1]
    slots = NB * NB
    given = (t_mats, struct_table, zone_atoms, zone_size, pair_index, zone_link, weights)
    bf16, f32 = jnp.bfloat16, jnp.float32
    green = pl.pallas_call(
        functools.partial(kernel, ne, na, adev),
        out_shape=jax.ShapeDtypeStruct((adev * ROWS, LANES), f32),
        in_specs=[pl.BlockSpec(memory_space=pltpu.HBM)] * len(given),
        out_specs=pl.BlockSpec(memory_space=pltpu.VMEM),
        scratch_shapes=[
            *[pltpu.VMEM(a.shape, a.dtype) for a in given[:2]],
            *[pltpu.SMEM(a.shape, a.dtype) for a in given[2:]],
            pltpu.VMEM((adev * ROWS, LANES), f32),
            pltpu.VMEM((na * adev + 1, ROWS, LANES), bf16),
            pltpu.VMEM((KTAB * ROWS, LANES), f32),
            pltpu.VMEM((KTAB, FORM, LANES), bf16),
            pltpu.VMEM((adev * (1 + NB), FORM, LANES), bf16),
            pltpu.VMEM((adev, KTAB + 1, L, FORM), f32),
            pltpu.VMEM((adev * slots * L, FORM), bf16),
            pltpu.VMEM((adev * slots * L, 256), bf16),
            pltpu.VMEM((adev * slots * L, FORM), bf16),
            pltpu.VMEM((ne * adev * ROWS, LANES), f32),
            pltpu.SemaphoreType.DMA((len(given),)),
            pltpu.SemaphoreType.DMA,
            pltpu.SemaphoreType.DMA,
            pltpu.SemaphoreType.DMA,
            pltpu.SemaphoreType.DMA,
        ],
        compiler_params=pltpu.CompilerParams(
            collective_id=0, has_side_effects=True, vmem_limit_bytes=32 * 1024 * 1024
        ),
    )(*given)
    return green.reshape(adev, 2 * L * L)


def solution(mesh):
    ne, na = mesh.shape["energy"], mesh.shape["atom"]
    return jax.shard_map(
        functools.partial(body, ne=ne, na=na),
        mesh=mesh,
        in_specs=(
            P("energy", "atom", None),
            P("energy", None, None),
            P("atom", None),
            P("atom"),
            P("atom", None),
            P("atom", None),
            P("energy", None),
        ),
        out_specs=P("atom", None),
        check_vma=False,
    )
```

time: 182 us -> 36.8 us (0.20)
  the two profiles are of different devices: /device:TPU:2 before, /device:TPU:1 now
where the time goes in v1:
time: 36.8 us; the launch traced here: 36.6 us
  Pallas kernels  31 us (84%)
  local copies, waits for them, and re-layouts  5.62 us (15%)
    pallas_call x1, Pallas kernels, body(): pl.pallas_call(functools.partial(kernel, ne, na, adev), out_shape=jax.Sha...  31 us
    unnamed x14, local copies, waits for them, and re-layouts  5 us

profile of v1, /device:TPU:1, one launch (start us, length us, event | category | flops | bytes accessed | tf_op | source)
XLA Modules:
  0.0 36.6 jit_solution(13872980028618368557)
XLA Ops:
  0.0 0.0 copy-start
  0.0 0.9 %copy-done = bf16[1,64,2048]{2,1,0:T(8,128)(2,1)S(1)} copy-done((bf16[1,64,2048]{2,1,0:T(8,128)(2,1)S(1)}, bf16[1,64,2048]{2,1,0:T(8,128)(2,1)}, u32[]{:S(2)}) %copy-start) | copy-done | bytes 262168
  1.0 0.0 copy-start.1
  1.0 0.7 %copy-done.1 = bf16[1,2,2048]{2,1,0:T(2,128)(2,1)S(1)} copy-done((bf16[1,2,2048]{2,1,0:T(2,128)(2,1)S(1)}, bf16[1,2,2048]{2,1,0:T(2,128)(2,1)}, u32[]{:S(2)}) %copy-start.1) | copy-done | bytes 8216
  1.6 0.0 copy-start.2
  1.7 0.7 %copy-done.2 = s32[2,384]{1,0:T(2,128)S(1)} copy-done((s32[2,384]{1,0:T(2,128)S(1)}, s32[2,384]{1,0:T(2,128)}, u32[]{:S(2)}) %copy-start.2) | copy-done | bytes 3096
  2.3 0.0 copy-start.3
  2.3 0.7 %copy-done.3 = s32[2,384]{1,0:T(2,128)S(1)} copy-done((s32[2,384]{1,0:T(2,128)S(1)}, s32[2,384]{1,0:T(2,128)}, u32[]{:S(2)}) %copy-start.3) | copy-done | bytes 3096
  3.0 0.0 copy-start.4
  3.0 0.7 %copy-done.4 = s32[2,64]{1,0:T(2,128)S(1)} copy-done((s32[2,64]{1,0:T(2,128)S(1)}, s32[2,64]{1,0:T(2,128)}, u32[]{:S(2)}) %copy-start.4) | copy-done | bytes 536
  3.7 0.0 copy-start.5
  3.7 0.7 %copy-done.5 = s32[2]{0:T(128)S(1)} copy-done((s32[2]{0:T(128)S(1)}, s32[2]{0:T(128)}, u32[]{:S(2)}) %copy-start.5) | copy-done | bytes 32
  4.4 0.0 copy-start.6
  4.4 0.7 %copy-done.6 = f32[1,2]{1,0:T(1,128)S(1)} copy-done((f32[1,2]{1,0:T(1,128)S(1)}, f32[1,2]{1,0:T(1,128)}, u32[]{:S(2)}) %copy-start.6) | copy-done | bytes 32
  5.0 31.0 %shard_map.73 = f32[32,128]{1,0:T(8,128)S(1)} custom-call(bf16[1,2,2048]{2,1,0:T(2,128)(2,1)S(1)} %copy-done.1, bf16[1,64,2048]{2,1,0:T(8,128)(2,1)S(1)} %copy-done, s32[2,64]{1,0:T(2,128)S(1)} %copy-done.4, s32[2]{0:T(128)S(1)} %copy-done.5, s32[2,384]{1,0:T(2,128)S(1)} %copy-done.2, s32[2,384]{1,0:T(2,128)S(1)} %copy-done.3, f32[1,2]{1,0:T(1,128)S(1)} %copy-done.6), custom_call_target="tpu_custom_call" | custom-call | tf_op jit(solution)/shard_map/pallas_call | solution.py:313
  36.0 0.6 %reshape.3 = f32[2,2048]{1,0:T(2,128)} reshape(f32[32,128]{1,0:T(8,128)S(1)} %shard_map.73) | data formatting | bytes 32768 | tf_op jit(solution)/shard_map/reshape | solution.py:341
Async XLA Ops:
  0.0 0.9 %copy-start = (bf16[1,64,2048]{2,1,0:T(8,128)(2,1)S(1)}, bf16[1,64,2048]{2,1,0:T(8,128)(2,1)}, u32[]{:S(2)}) copy-start(bf16[1,64,2048]{2,1,0:T(8,128)(2,1)} %tab_hbm.1) | copy-start | bytes 786436
  1.0 0.7 %copy-start.1 = (bf16[1,2,2048]{2,1,0:T(2,128)(2,1)S(1)}, bf16[1,2,2048]{2,1,0:T(2,128)(2,1)}, u32[]{:S(2)}) copy-start(bf16[1,2,2048]{2,1,0:T(2,128)(2,1)} %t_hbm.1) | copy-start | bytes 24580
  1.6 0.7 %copy-start.2 = (s32[2,384]{1,0:T(2,128)S(1)}, s32[2,384]{1,0:T(2,128)}, u32[]{:S(2)}) copy-start(s32[2,384]{1,0:T(2,128)} %pair_hbm.1) | copy-start | bytes 9220
  2.3 0.7 %copy-start.3 = (s32[2,384]{1,0:T(2,128)S(1)}, s32[2,384]{1,0:T(2,128)}, u32[]{:S(2)}) copy-start(s32[2,384]{1,0:T(2,128)} %link_hbm.1) | copy-start | bytes 9220
  3.0 0.7 %copy-start.4 = (s32[2,64]{1,0:T(2,128)S(1)}, s32[2,64]{1,0:T(2,128)}, u32[]{:S(2)}) copy-start(s32[2,64]{1,0:T(2,128)} %atoms_hbm.1) | copy-start | bytes 1540
  3.7 0.7 %copy-start.5 = (s32[2]{0:T(128)S(1)}, s32[2]{0:T(128)}, u32[]{:S(2)}) copy-start(s32[2]{0:T(128)} %size_hbm.1) | copy-start | bytes 28
  4.4 0.7 %copy-start.6 = (f32[1,2]{1,0:T(1,128)S(1)}, f32[1,2]{1,0:T(1,128)}, u32[]{:S(2)}) copy-start(f32[1,2]{1,0:T(1,128)} %w_hbm.1) | copy-start | bytes 28

commit v2 on v1

--- a/solution.py
+++ b/solution.py
@@ -44,18 +44,12 @@
     )
 
 
-def spread_matrix():
-    i = iota2((64, 256), 0)
-    j = iota2((64, 256), 1)
+def start_matrix():
+    k = iota2((L, LANES), 0)
+    l = iota2((L, LANES), 1)
     return to_bf16_mask(
-        (((i >> 3) & 1) == (j >> 7)) & (((i & 7) * 4 + (i >> 4)) == (j & 31))
+        (l < FORM) & (((l >> 3) & 1) == 0) & (((l & 7) * 4 + (l >> 4)) == k)
     )
-
-
-def start_matrix():
-    k = iota2((L, FORM), 0)
-    l = iota2((L, FORM), 1)
-    return to_bf16_mask((((l >> 3) & 1) == 0) & (((l & 7) * 4 + (l >> 4)) == k))
 
 
 def partner(x):
@@ -75,7 +69,7 @@
     t_hbm, tab_hbm, atoms_hbm, size_hbm, pair_hbm, link_hbm, w_hbm,
     out_ref,
     t_ref, tab_ref, atoms, size, pair, link, w_ref,
-    xf, gath, tabx, gform, tform, pbuf, c1, c1rep, near, arbuf,
+    xf, gath, tabx, gform, own_form, tform, pbuf, c1, near1, near2, wide, arbuf,
     in_sems, ag_send, ag_recv, ar_send, ar_recv,
 ):
     e = lax.axis_index("energy")
@@ -157,14 +151,17 @@
         return 0
 
     lax.fori_loop(0, KTAB // 8, table_forms, 0)
-    put_forms(tform, 0, with_partner(own32))
+    put_forms(own_form, 0, with_partner(own32))
 
     def form(ref, k):
-        return ref[k][:, :FORM]
+        return ref[k]
 
     sel = start_matrix()
-    start = [dot_nt(sel, form(tform, z)) for z in range(adev)]
-    start_all = jnp.concatenate(start, axis=0).astype(jnp.bfloat16)
+    start = [dot_nt(sel, form(own_form, z)) for z in range(adev)]
+    wide[...] = jnp.zeros_like(wide)
+    for z in range(adev):
+        wide[z * L : (z + 1) * L, :FORM] = start[z].astype(jnp.bfloat16)
+    start_all = wide[0 : adev * L, :]
 
     def table_times_start(i, _):
         for k in range(8):
@@ -181,6 +178,8 @@
     slots = NB * NB
     for copy in loads[2:]:
         copy.wait()
+    for buf in (c1, near1, near2):
+        buf[...] = jnp.zeros_like(buf)
     for z in range(adev):
 
         def first_coupled(n, _, z=z):
@@ -192,28 +191,17 @@
                     at = a * NB + j
                     term = pbuf[z, jnp.minimum(pair[z, at] + link[z, at] * KTAB, KTAB)]
                     acc = term if acc is None else acc + term
-                c1[pl.ds(pl.multiple_of((z * slots + n * NB + m) * L, L), L), :] = acc.astype(
+                c1[pl.ds(pl.multiple_of((z * slots + n * NB + m) * L, L), L), :FORM] = acc.astype(
                     jnp.bfloat16
                 )
             return 0
 
         lax.fori_loop(0, NB, first_coupled, 0)
 
-    rep = spread_matrix()
-
-    def spread(i, _):
-        rows = pl.ds(pl.multiple_of(i * 256, 256), 256)
-        c1rep[rows, :] = dot(c1[rows, :], rep).astype(jnp.bfloat16)
-        return 0
-
-    lax.fori_loop(0, adev * slots * L // 256, spread, 0)
-
     others = gath.at[pl.ds(0, (na - 1) * adev)]
     pltpu.make_async_copy(others, others, ag_recv).wait()
     pltpu.make_async_copy(others, others, ag_send).wait()
 
-    lane_group = iota2((ROWS, LANES), 1) >> 5
-
     def member(z, a):
         absent = jnp.maximum(a - size[z] + 1, 0)
         return jnp.minimum(atoms[z, a] + absent * n_atoms, n_atoms)
@@ -221,65 +209,54 @@
     def is_first(a):
         return 1.0 - jnp.minimum(a, 1).astype(jnp.float32)
 
-    def packed(atom):
-        return gath[atom]
-
-    def wide_form(x):
-        x32 = x.astype(jnp.float32)
-        y32 = jnp.concatenate([-x32[8:], x32[:8]], axis=0)
-
-        def groups(v):
-            return jnp.concatenate(
-                [jnp.where(lane_group == s, v, 0.0).astype(jnp.bfloat16) for s in range(4)],
-                axis=0,
-            )
-
-        return jnp.concatenate([groups(x32), groups(y32)], axis=1)
-
-    for z in range(adev):
-        x32 = jnp.concatenate(
-            [packed(member(z, link[z, n])) for n in range(NB)], axis=0
-        ).astype(jnp.float32)
-        put_forms(tform, adev + z * NB, with_partner(x32))
-
-    for z in range(adev):
-
-        def first_column(n, _, z=z):
-            b = link[z, n]
-            for m in range(NB):
-                a = link[z, b * NB + m]
-                at = pl.ds(pl.multiple_of((z * slots + n * NB + m) * L, L), L)
-                col = dot_nt(c1rep[at, :], wide_form(packed(member(z, a))))
-                col = col + is_first(a) * start[z]
-                near[at, :] = col.astype(jnp.bfloat16)
-            return 0
-
-        lax.fori_loop(0, NB, first_column, 0)
-
-    lane_group_f = iota2((ROWS, LANES), 1) >> 5
+    tform[n_atoms] = jnp.zeros((FORM, LANES), jnp.bfloat16)
+    step = min(16, n_atoms)
+
+    def all_forms(i, _):
+        rows = gath[pl.ds(i * step, step)].reshape(step * ROWS, LANES)
+        put_forms(tform, i * step, with_partner(rows.astype(jnp.float32)))
+        return 0
+
+    lax.fori_loop(0, n_atoms // step, all_forms, 0)
+
+    zn = [(z, n) for z in range(adev) for n in range(NB)]
+    slot = {(z, n): link[z, n] for z, n in zn}
+
+    for i, (z, n) in enumerate(zn):
+        for m in range(NB):
+            a = link[z, slot[z, n] * NB + m]
+            at = (i * NB + m) * L
+            col = dot_nt(c1[at : at + L, :], form(tform, member(z, a)))
+            col = col + is_first(a) * start[z]
+            near1[i * L : (i + 1) * L, m * LANES : m * LANES + FORM] = col.astype(jnp.bfloat16)
+
+    for i, (z, n) in enumerate(zn):
+        g = jnp.concatenate(
+            [form(gform, pair[z, slot[z, n] * NB + m]) for m in range(NB)], axis=1
+        )
+        coupled = dot_nt(near1[i * L : (i + 1) * L, :], g)
+        wide[i * L : (i + 1) * L, :FORM] = coupled.astype(jnp.bfloat16)
+    for i, (z, n) in enumerate(zn):
+        b = slot[z, n]
+        col = dot_nt(wide[i * L : (i + 1) * L, :], form(tform, member(z, b)))
+        col = col + is_first(b) * start[z]
+        near2[z * L : (z + 1) * L, n * LANES : n * LANES + FORM] = col.astype(jnp.bfloat16)
+
+    for z in range(adev):
+        g = jnp.concatenate([form(gform, pair[z, n]) for n in range(NB)], axis=1)
+        coupled = dot_nt(near2[z * L : (z + 1) * L, :], g)
+        wide[z * L : (z + 1) * L, :FORM] = coupled.astype(jnp.bfloat16)
+
+    lane_group = iota2((ROWS, LANES), 1) >> 5
     w_re = w_ref[0, 0]
     w_im = w_ref[0, 1]
     mine = pl.multiple_of(e * blk, blk)
     for z in range(adev):
-        total = None
-        for n in range(NB):
-            b = link[z, n]
-            acc = None
-            for m in range(NB):
-                at = (z * slots + n * NB + m) * L
-                term = dot_nt(near[at : at + L, :], form(gform, pair[z, b * NB + m]))
-                acc = term if acc is None else acc + term
-            col = dot_nt(acc.astype(jnp.bfloat16), form(tform, adev + z * NB + n))
-            col = col + is_first(b) * start[z]
-            term = dot_nt(col.astype(jnp.bfloat16), form(gform, pair[z, n]))
-            total = term if total is None else total + term
-        coupled = total.astype(jnp.bfloat16)
-        diag = dot_nt(form(tform, z), jnp.concatenate([coupled] * 4, axis=0))
+        coupled = wide[z * L : (z + 1) * L, :]
+        diag = dot_nt(form(own_form, z), jnp.concatenate([coupled] * 4, axis=0))
         block = xf[z * ROWS : (z + 1) * ROWS, :]
         for s in range(4):
-            block = block + jnp.where(
-                lane_group_f == s, diag[s * ROWS : (s + 1) * ROWS, :], 0.0
-            )
+            block = block + jnp.where(lane_group == s, diag[s * ROWS : (s + 1) * ROWS, :], 0.0)
         re, im = block[:8], block[8:]
         arbuf[pl.ds(mine + z * ROWS, 8), :] = w_re * re - w_im * im
         arbuf[pl.ds(mine + z * ROWS + 8, 8), :] = w_re * im + w_im * re
@@ -322,11 +299,13 @@
             pltpu.VMEM((na * adev + 1, ROWS, LANES), bf16),
             pltpu.VMEM((KTAB * ROWS, LANES), f32),
             pltpu.VMEM((KTAB, FORM, LANES), bf16),
-            pltpu.VMEM((adev * (1 + NB), FORM, LANES), bf16),
+            pltpu.VMEM((adev, FORM, LANES), bf16),
+            pltpu.VMEM((na * adev + 1, FORM, LANES), bf16),
             pltpu.VMEM((adev, KTAB + 1, L, FORM), f32),
-            pltpu.VMEM((adev * slots * L, FORM), bf16),
-            pltpu.VMEM((adev * slots * L, 256), bf16),
-            pltpu.VMEM((adev * slots * L, FORM), bf16),
+            pltpu.VMEM((adev * slots * L, LANES), bf16),
+            pltpu.VMEM((adev * NB * L, NB * LANES), bf16),
+            pltpu.VMEM((adev * L, NB * LANES), bf16),
+            pltpu.VMEM((adev * NB * L, LANES), bf16),
             pltpu.VMEM((ne * adev * ROWS, LANES), f32),
             pltpu.SemaphoreType.DMA((len(given),)),
             pltpu.SemaphoreType.DMA,
@@ -337,7 +316,7 @@
         compiler_params=pltpu.CompilerParams(
             collective_id=0, has_side_effects=True, vmem_limit_bytes=32 * 1024 * 1024
         ),
-    )(*given)
+    )(*[pltpu.with_memory_space_constraint(a, pltpu.HBM) for a in given])
     return green.reshape(adev, 2 * L * L)
 
 

time: 36.8 us -> 25.3 us (0.69)
  Pallas kernels: 31 us -> 24.6 us
  local copies, waits for them, and re-layouts: 5.62 us -> 0.62 us
    pallas_call x1, Pallas kernels: 31 us -> 24.6 us  [body(): pl.pallas_call(functools.partial(kernel, ne, na, adev), out_shape=jax.Sha...]
    unnamed x14 -> x0, local copies, waits for them, and re-layouts: 5 us -> none
where the time goes in v2:
time: 25.3 us; the launch traced here: 25.2 us
  Pallas kernels  24.6 us (97%)
  local copies, waits for them, and re-layouts  0.62 us (2%)
    pallas_call x1, Pallas kernels, body(): pl.pallas_call(functools.partial(kernel, ne, na, adev), out_shape=jax.Sha...  24.6 us
    reshape x1, local copies, waits for them, and re-layouts, body(): return green.reshape(adev, 2 * L * L)  0.62 us

profile of v2, /device:TPU:1, one launch (start us, length us, event | category | flops | bytes accessed | tf_op | source)
XLA Modules:
  0.0 25.2 jit_solution(4163145539899638205)
XLA Ops:
  0.0 24.6 %shard_map.73 = f32[32,128]{1,0:T(8,128)S(1)} custom-call(bf16[1,2,2048]{2,1,0:T(2,128)(2,1)} %t_hbm.1, bf16[1,64,2048]{2,1,0:T(8,128)(2,1)} %tab_hbm.1, s32[2,64]{1,0:T(2,128)} %atoms_hbm.1, s32[2]{0:T(128)} %size_hbm.1, s32[2,384]{1,0:T(2,128)} %pair_hbm.1, s32[2,384]{1,0:T(2,128)} %link_hbm.1, f32[1,2]{1,0:T(1,128)} %w_hbm.1), custom_call_target="tpu_custom_call" | custom-call | tf_op jit(solution)/shard_map/pallas_call | solution.py:290
  24.6 0.6 %reshape.3 = f32[2,2048]{1,0:T(2,128)} reshape(f32[32,128]{1,0:T(8,128)S(1)} %shard_map.73) | data formatting | bytes 32768 | tf_op jit(solution)/shard_map/reshape | solution.py:320

commit v3 on v2

--- a/solution.py
+++ b/solution.py
@@ -62,6 +62,16 @@
     return jnp.concatenate(
         [x32.astype(jnp.bfloat16), partner(x32).astype(jnp.bfloat16)], axis=1
     )
+
+
+def ring(d, n):
+    return min(d % n, -d % n)
+
+
+def grid_of(na):
+    chips = na // 2
+    nx = max(d for d in range(1, chips + 1) if chips % d == 0 and d * d <= chips)
+    return nx, chips // nx
 
 
 def kernel(
@@ -86,22 +96,46 @@
     for copy in loads:
         copy.start()
 
+    nx, ny = grid_of(na)
+    core = lax.rem(me, 2)
+    chip = lax.div(me, 2)
+    x, y = lax.div(chip, ny), lax.rem(chip, ny)
+    hops = {
+        (dx, dy): ring(dx, nx) + ring(dy, ny)
+        for dx in range(nx)
+        for dy in range(ny)
+        if dx + dy > 0
+    }
+    offsets = sorted(hops, key=lambda o: -hops[o])
+    split = max(hops.values()) // 2
+    groups = [
+        [o for o in offsets if hops[o] > split],
+        [o for o in offsets if 1 < hops[o] <= split],
+        [o for o in offsets if hops[o] == 1],
+    ]
+    slot_of = {o: i for i, o in enumerate([(0, 0)] + offsets)}
+    n_slots = len(slot_of)
+
+    def chip_at(o):
+        return lax.rem(x + o[0], nx) * ny + lax.rem(y + o[1], ny)
+
+    def device_at(o, other):
+        return (e, chip_at(o) * 2 + (1 - core if other else core))
+
+    sibling = device_at((0, 0), True)
+    energies = sorted(range(1, ne), key=lambda d: -ring(d, ne))
+
     barrier = pltpu.get_barrier_semaphore()
 
-    def greet_atom(d, _):
-        pl.semaphore_signal(
-            barrier, inc=1, device_id=(e, lax.rem(me + d, na)), device_id_type=MESH
-        )
-        return 0
-
-    def greet_energy(d, _):
-        pl.semaphore_signal(
-            barrier, inc=1, device_id=(lax.rem(e + d, ne), me), device_id_type=MESH
-        )
-        return 0
-
-    lax.fori_loop(1, na, greet_atom, 0)
-    lax.fori_loop(1, ne, greet_energy, 0)
+    def greet(device):
+        pl.semaphore_signal(barrier, inc=1, device_id=device, device_id_type=MESH)
+
+    for d in energies:
+        greet((lax.rem(e + d, ne), me))
+    for o in offsets:
+        greet(device_at(o, False))
+        greet(device_at(o, True))
+    greet(sibling)
 
     loads[0].wait()
     for t in range(ROWS):
@@ -110,25 +144,32 @@
         ].astype(jnp.float32)
     own32 = xf[...]
     own = own32.astype(jnp.bfloat16)
-    my_rows = pl.ds(me * adev, adev)
-    for z in range(adev):
-        gath[me * adev + z] = own[z * ROWS : (z + 1) * ROWS]
-    gath[n_atoms] = jnp.zeros((ROWS, LANES), jnp.bfloat16)
+    mine_at = core * n_slots
+    for z in range(adev):
+        gath[mine_at, z] = own[z * ROWS : (z + 1) * ROWS]
 
     pl.semaphore_wait(barrier, na - 1 + ne - 1)
 
-    def send(d, _):
+    def wait_blocks(count, sem):
+        blocks = gath.at[pl.ds(0, count)]
+        pltpu.make_async_copy(blocks, blocks, sem).wait()
+
+    def send(o, other, sem):
+        dst = core * n_slots + slot_of[-o[0] % nx, -o[1] % ny]
         pltpu.make_async_remote_copy(
-            src_ref=gath.at[my_rows],
-            dst_ref=gath.at[my_rows],
+            src_ref=gath.at[mine_at],
+            dst_ref=gath.at[dst],
             send_sem=ag_send,
-            recv_sem=ag_recv,
-            device_id=(e, lax.rem(me + d, na)),
+            recv_sem=sem,
+            device_id=device_at(o, other),
             device_id_type=MESH,
         ).start()
-        return 0
-
-    lax.fori_loop(1, na, send, 0)
+
+    for i, group in enumerate(groups):
+        for o in group:
+            send(o, True, ag_recv.at[i])
+            send(o, False, ag_recv.at[i])
+    send((0, 0), True, ag_recv.at[len(groups)])
 
     ab = form_matrix()
     loads[1].wait()
@@ -150,7 +191,7 @@
         put_forms(gform, i * 8, with_partner(rows))
         return 0
 
-    lax.fori_loop(0, KTAB // 8, table_forms, 0)
+    lax.fori_loop(0, KTAB // 8, table_forms, 0, unroll=4)
     put_forms(own_form, 0, with_partner(own32))
 
     def form(ref, k):
@@ -171,7 +212,7 @@
                 pbuf[z, b] = term[z * L : (z + 1) * L]
         return 0
 
-    lax.fori_loop(0, KTAB // 8, table_times_start, 0)
+    lax.fori_loop(0, KTAB // 8, table_times_start, 0, unroll=4)
     for z in range(adev):
         pbuf[z, KTAB] = jnp.zeros((L, FORM), jnp.float32)
 
@@ -196,11 +237,38 @@
                 )
             return 0
 
-        lax.fori_loop(0, NB, first_coupled, 0)
-
-    others = gath.at[pl.ds(0, (na - 1) * adev)]
-    pltpu.make_async_copy(others, others, ag_recv).wait()
-    pltpu.make_async_copy(others, others, ag_send).wait()
+        lax.fori_loop(0, NB, first_coupled, 0, unroll=NB)
+
+    tform[n_atoms] = jnp.zeros((FORM, LANES), jnp.bfloat16)
+
+    def forms_of(blocks):
+        for first in range(0, len(blocks), 8):
+            some = blocks[first : first + 8]
+            rows = jnp.concatenate(
+                [
+                    gath[(1 - core if other else core) * n_slots + slot_of[o]].reshape(
+                        adev * ROWS, LANES
+                    )
+                    for o, other in some
+                ],
+                axis=0,
+            )
+            forms = dot(with_partner(rows.astype(jnp.float32)), ab).astype(jnp.bfloat16)
+            for i, (o, other) in enumerate(some):
+                owner = chip_at(o) * 2 + (1 - core if other else core)
+                for k in range(adev):
+                    at = (i * adev + k) * ROWS
+                    for s in range(4):
+                        tform[owner * adev + k, s * ROWS : (s + 1) * ROWS, :] = forms[
+                            at : at + ROWS, s * LANES : (s + 1) * LANES
+                        ]
+
+    wait_blocks(1, ag_recv.at[len(groups)])
+    forms_of([((0, 0), False), ((0, 0), True)])
+    for i, group in reversed(list(enumerate(groups))):
+        if group:
+            wait_blocks(2 * len(group), ag_recv.at[i])
+            forms_of([(o, other) for o in group for other in (False, True)])
 
     def member(z, a):
         absent = jnp.maximum(a - size[z] + 1, 0)
@@ -208,16 +276,6 @@
 
     def is_first(a):
         return 1.0 - jnp.minimum(a, 1).astype(jnp.float32)
-
-    tform[n_atoms] = jnp.zeros((FORM, LANES), jnp.bfloat16)
-    step = min(16, n_atoms)
-
-    def all_forms(i, _):
-        rows = gath[pl.ds(i * step, step)].reshape(step * ROWS, LANES)
-        put_forms(tform, i * step, with_partner(rows.astype(jnp.float32)))
-        return 0
-
-    lax.fori_loop(0, n_atoms // step, all_forms, 0)
 
     zn = [(z, n) for z in range(adev) for n in range(NB)]
     slot = {(z, n): link[z, n] for z, n in zn}
@@ -261,7 +319,7 @@
         arbuf[pl.ds(mine + z * ROWS, 8), :] = w_re * re - w_im * im
         arbuf[pl.ds(mine + z * ROWS + 8, 8), :] = w_re * im + w_im * re
 
-    def share(d, _):
+    for d in energies:
         pltpu.make_async_remote_copy(
             src_ref=arbuf.at[pl.ds(mine, blk)],
             dst_ref=arbuf.at[pl.ds(mine, blk)],
@@ -270,9 +328,6 @@
             device_id=(lax.rem(e + d, ne), me),
             device_id_type=MESH,
         ).start()
-        return 0
-
-    lax.fori_loop(1, ne, share, 0)
     rest = arbuf.at[pl.ds(0, (ne - 1) * blk)]
     pltpu.make_async_copy(rest, rest, ar_recv).wait()
     pltpu.make_async_copy(rest, rest, ar_send).wait()
@@ -280,6 +335,7 @@
     for i in range(1, ne):
         green = green + arbuf[i * blk : (i + 1) * blk, :]
     out_ref[...] = green
+    wait_blocks(na - 1, ag_send)
 
 
 def body(t_mats, struct_table, zone_atoms, zone_size, pair_index, zone_link, weights, ne, na):
@@ -296,7 +352,7 @@
             *[pltpu.VMEM(a.shape, a.dtype) for a in given[:2]],
             *[pltpu.SMEM(a.shape, a.dtype) for a in given[2:]],
             pltpu.VMEM((adev * ROWS, LANES), f32),
-            pltpu.VMEM((na * adev + 1, ROWS, LANES), bf16),
+            pltpu.VMEM((na, adev, ROWS, LANES), bf16),
             pltpu.VMEM((KTAB * ROWS, LANES), f32),
             pltpu.VMEM((KTAB, FORM, LANES), bf16),
             pltpu.VMEM((adev, FORM, LANES), bf16),
@@ -309,7 +365,7 @@
             pltpu.VMEM((ne * adev * ROWS, LANES), f32),
             pltpu.SemaphoreType.DMA((len(given),)),
             pltpu.SemaphoreType.DMA,
-            pltpu.SemaphoreType.DMA,
+            pltpu.SemaphoreType.DMA((4,)),
             pltpu.SemaphoreType.DMA,
             pltpu.SemaphoreType.DMA,
         ],

time: 25.3 us -> 22.9 us (0.905)
  Pallas kernels: 24.6 us -> 22.1 us
    pallas_call x1, Pallas kernels: 24.6 us -> 22.1 us  [body(): pl.pallas_call(functools.partial(kernel, ne, na, adev), out_shape=jax.Sha...]
where the time goes in v3:
time: 22.9 us; the launch traced here: 22.7 us
  Pallas kernels  22.1 us (97%)
  local copies, waits for them, and re-layouts  0.62 us (3%)
    pallas_call x1, Pallas kernels, body(): pl.pallas_call(functools.partial(kernel, ne, na, adev), out_shape=jax.Sha...  22.1 us
    reshape x1, local copies, waits for them, and re-layouts, body(): return green.reshape(adev, 2 * L * L)  0.62 us

profile of v3, /device:TPU:1, one launch (start us, length us, event | category | flops | bytes accessed | tf_op | source)
XLA Modules:
  0.0 22.7 jit_solution(16219998821020180294)
XLA Ops:
  0.0 22.1 %shard_map.73 = f32[32,128]{1,0:T(8,128)S(1)} custom-call(bf16[1,2,2048]{2,1,0:T(2,128)(2,1)} %t_hbm.1, bf16[1,64,2048]{2,1,0:T(8,128)(2,1)} %tab_hbm.1, s32[2,64]{1,0:T(2,128)} %atoms_hbm.1, s32[2]{0:T(128)} %size_hbm.1, s32[2,384]{1,0:T(2,128)} %pair_hbm.1, s32[2,384]{1,0:T(2,128)} %link_hbm.1, f32[1,2]{1,0:T(1,128)} %w_hbm.1), custom_call_target="tpu_custom_call" | custom-call | tf_op jit(solution)/shard_map/pallas_call | solution.py:346
  22.1 0.6 %reshape.3 = f32[2,2048]{1,0:T(2,128)} reshape(f32[32,128]{1,0:T(8,128)S(1)} %shard_map.73) | data formatting | bytes 32768 | tf_op jit(solution)/shard_map/reshape | solution.py:376

commit v4 on v3

--- a/solution.py
+++ b/solution.py
@@ -38,9 +38,9 @@
     i = iota2((256, 512), 0)
     j = iota2((256, 512), 1)
     h, s1, c = i >> 7, (i >> 5) & 3, i & 31
-    s, l = j >> 7, j & 127
+    s, l = j >> 7, j & 63
     return to_bf16_mask(
-        (s1 == s) & (l < 64) & (((l >> 3) & 1) == h) & (((l & 7) * 4 + (l >> 4)) == c)
+        (s1 == s) & (((l >> 3) & 1) == h) & (((l & 7) * 4 + (l >> 4)) == c)
     )
 
 
@@ -78,17 +78,24 @@
     ne, na, adev,
     t_hbm, tab_hbm, atoms_hbm, size_hbm, pair_hbm, link_hbm, w_hbm,
     out_ref,
-    t_ref, tab_ref, atoms, size, pair, link, w_ref,
-    xf, gath, tabx, gform, own_form, tform, pbuf, c1, near1, near2, wide, arbuf,
-    in_sems, ag_send, ag_recv, ar_send, ar_recv,
+    t_ref, tab_ref, size, w_ref, *scratch,
 ):
+    link, pair, atoms = (scratch[i * adev : (i + 1) * adev] for i in range(3))
+    (
+        t_at, g_at, first_at,
+        xf, gath, tabx, gform, own_form, tform, pbuf, start4, c1, near1, c2, near2, c3, arbuf,
+        in_sems, ag_send, ag_recv, ar_send, ar_recv,
+    ) = scratch[3 * adev :]
     e = lax.axis_index("energy")
     me = lax.axis_index("atom")
     n_atoms = na * adev
     blk = adev * ROWS
 
-    sources = (t_hbm, tab_hbm, link_hbm, pair_hbm, atoms_hbm, size_hbm, w_hbm)
-    landed = (t_ref, tab_ref, link, pair, atoms, size, w_ref)
+    sources = [t_hbm, tab_hbm, size_hbm, w_hbm]
+    landed = [t_ref, tab_ref, size, w_ref]
+    for z in range(adev):
+        sources += [link_hbm.at[z], pair_hbm.at[z], atoms_hbm.at[z]]
+        landed += [link[z], pair[z], atoms[z]]
     loads = [
         pltpu.make_async_copy(src, dst, in_sems.at[i])
         for i, (src, dst) in enumerate(zip(sources, landed))
@@ -107,11 +114,8 @@
         if dx + dy > 0
     }
     offsets = sorted(hops, key=lambda o: -hops[o])
-    split = max(hops.values()) // 2
     groups = [
-        [o for o in offsets if hops[o] > split],
-        [o for o in offsets if 1 < hops[o] <= split],
-        [o for o in offsets if hops[o] == 1],
+        [o for o in offsets if hops[o] == h] for h in range(max(hops.values()), 0, -1)
     ]
     slot_of = {o: i for i, o in enumerate([(0, 0)] + offsets)}
     n_slots = len(slot_of)
@@ -199,45 +203,71 @@
 
     sel = start_matrix()
     start = [dot_nt(sel, form(own_form, z)) for z in range(adev)]
-    wide[...] = jnp.zeros_like(wide)
-    for z in range(adev):
-        wide[z * L : (z + 1) * L, :FORM] = start[z].astype(jnp.bfloat16)
-    start_all = wide[0 : adev * L, :]
+    for buf in (start4, c1, c2, c3):
+        buf[...] = jnp.zeros_like(buf)
+    for q in range(4):
+        for z in range(adev):
+            at = (q * adev + z) * L
+            start4[at : at + L, q * FORM : (q + 1) * FORM] = start[z].astype(jnp.bfloat16)
+
+    low = iota2((FORM, LANES), 1) < FORM
+
+    def side_by_side(forms):
+        return jnp.concatenate(
+            [
+                jnp.where(low, forms[i], forms[i + 1])
+                for i in range(0, len(forms), 2)
+            ],
+            axis=1,
+        )
 
     def table_times_start(i, _):
-        for k in range(8):
-            b = i * 8 + k
-            term = dot_nt(start_all, form(gform, b))
-            for z in range(adev):
-                pbuf[z, b] = term[z * L : (z + 1) * L]
+        for j in range(2):
+            k = i * 8 + j * 4
+            terms = dot_nt(
+                start4[...], side_by_side([form(gform, k + q) for q in range(4)])
+            )
+            for q in range(4):
+                for z in range(adev):
+                    at = (q * adev + z) * L
+                    pbuf[z, k + q] = terms[at : at + L]
         return 0
 
     lax.fori_loop(0, KTAB // 8, table_times_start, 0, unroll=4)
     for z in range(adev):
         pbuf[z, KTAB] = jnp.zeros((L, FORM), jnp.float32)
 
-    slots = NB * NB
     for copy in loads[2:]:
         copy.wait()
-    for buf in (c1, near1, near2):
-        buf[...] = jnp.zeros_like(buf)
-    for z in range(adev):
-
-        def first_coupled(n, _, z=z):
-            b = link[z, n]
-            for m in range(NB):
-                a = link[z, b * NB + m]
-                acc = None
-                for j in range(NB):
-                    at = a * NB + j
-                    term = pbuf[z, jnp.minimum(pair[z, at] + link[z, at] * KTAB, KTAB)]
-                    acc = term if acc is None else acc + term
-                c1[pl.ds(pl.multiple_of((z * slots + n * NB + m) * L, L), L), :FORM] = acc.astype(
-                    jnp.bfloat16
-                )
-            return 0
-
-        lax.fori_loop(0, NB, first_coupled, 0, unroll=NB)
+    wanted = [(z, n, m) for z in range(adev) for n in range(NB) for m in range(NB)]
+    zn = [(z, n) for z in range(adev) for n in range(NB)]
+
+    def block(i):
+        row = (i // 4) * 4 * L + (i % 4) * L
+        return slice(row, row + L), slice((i % 4) * FORM, (i % 4 + 1) * FORM)
+
+    def member(z, a):
+        absent = jnp.maximum(a - size[z] + 1, 0)
+        return jnp.minimum(atoms[z][a] + absent * n_atoms, n_atoms)
+
+    def note(i, z, a, at):
+        t_at[i] = member(z, a)
+        g_at[i] = pair[z][at]
+        first_at[i] = 1.0 - jnp.minimum(a, 1).astype(jnp.float32)
+
+    for i, (z, n, m) in enumerate(wanted):
+        link_at = link[z][n] * NB + m
+        a = link[z][link_at]
+        note(i, z, a, link_at)
+        acc = None
+        for j in range(NB):
+            at = a * NB + j
+            term = pbuf[z, jnp.minimum(pair[z][at] + link[z][at] * KTAB, KTAB)]
+            acc = term if acc is None else acc + term
+        c1[block(i)] = acc.astype(jnp.bfloat16)
+    inner = len(wanted)
+    for i, (z, n) in enumerate(zn):
+        note(inner + i, z, link[z][n], n)
 
     tform[n_atoms] = jnp.zeros((FORM, LANES), jnp.bfloat16)
 
@@ -265,57 +295,52 @@
 
     wait_blocks(1, ag_recv.at[len(groups)])
     forms_of([((0, 0), False), ((0, 0), True)])
-    for i, group in reversed(list(enumerate(groups))):
+    for i, group in enumerate(groups):
         if group:
             wait_blocks(2 * len(group), ag_recv.at[i])
             forms_of([(o, other) for o in group for other in (False, True)])
 
-    def member(z, a):
-        absent = jnp.maximum(a - size[z] + 1, 0)
-        return jnp.minimum(atoms[z, a] + absent * n_atoms, n_atoms)
-
-    def is_first(a):
-        return 1.0 - jnp.minimum(a, 1).astype(jnp.float32)
-
-    zn = [(z, n) for z in range(adev) for n in range(NB)]
-    slot = {(z, n): link[z, n] for z, n in zn}
-
-    for i, (z, n) in enumerate(zn):
-        for m in range(NB):
-            a = link[z, slot[z, n] * NB + m]
-            at = (i * NB + m) * L
-            col = dot_nt(c1[at : at + L, :], form(tform, member(z, a)))
-            col = col + is_first(a) * start[z]
-            near1[i * L : (i + 1) * L, m * LANES : m * LANES + FORM] = col.astype(jnp.bfloat16)
-
-    for i, (z, n) in enumerate(zn):
-        g = jnp.concatenate(
-            [form(gform, pair[z, slot[z, n] * NB + m]) for m in range(NB)], axis=1
+    def columns(states, first, base):
+        at = base + first
+        forms = side_by_side([form(tform, t_at[at + q]) for q in range(4)])
+        cols = dot_nt(states[first * L : (first + 4) * L, :], forms)
+        return [(cols[q * L : (q + 1) * L], first_at[at + q]) for q in range(4)]
+
+    for first in range(0, inner, 4):
+        for q, (col, here) in enumerate(columns(c1, first, 0)):
+            z, n, m = wanted[first + q]
+            at = (z * NB + n) * L
+            near1[at : at + L, m * FORM : (m + 1) * FORM] = (col + here * start[z]).astype(
+                jnp.bfloat16
+            )
+
+    for i in range(len(zn)):
+        g = side_by_side([form(gform, g_at[i * NB + m]) for m in range(NB)])
+        c2[block(i)] = dot_nt(near1[i * L : (i + 1) * L, :], g).astype(jnp.bfloat16)
+    for first in range(0, len(zn), 4):
+        for q, (col, here) in enumerate(columns(c2, first, inner)):
+            z, n = zn[first + q]
+            near2[z * L : (z + 1) * L, n * FORM : (n + 1) * FORM] = (
+                col + here * start[z]
+            ).astype(jnp.bfloat16)
+
+    for z in range(adev):
+        g = side_by_side([form(gform, g_at[inner + z * NB + n]) for n in range(NB)])
+        c3[z * L : (z + 1) * L, :FORM] = dot_nt(near2[z * L : (z + 1) * L, :], g).astype(
+            jnp.bfloat16
         )
-        coupled = dot_nt(near1[i * L : (i + 1) * L, :], g)
-        wide[i * L : (i + 1) * L, :FORM] = coupled.astype(jnp.bfloat16)
-    for i, (z, n) in enumerate(zn):
-        b = slot[z, n]
-        col = dot_nt(wide[i * L : (i + 1) * L, :], form(tform, member(z, b)))
-        col = col + is_first(b) * start[z]
-        near2[z * L : (z + 1) * L, n * LANES : n * LANES + FORM] = col.astype(jnp.bfloat16)
-
-    for z in range(adev):
-        g = jnp.concatenate([form(gform, pair[z, n]) for n in range(NB)], axis=1)
-        coupled = dot_nt(near2[z * L : (z + 1) * L, :], g)
-        wide[z * L : (z + 1) * L, :FORM] = coupled.astype(jnp.bfloat16)
 
     lane_group = iota2((ROWS, LANES), 1) >> 5
     w_re = w_ref[0, 0]
     w_im = w_ref[0, 1]
     mine = pl.multiple_of(e * blk, blk)
     for z in range(adev):
-        coupled = wide[z * L : (z + 1) * L, :]
+        coupled = c3[z * L : (z + 1) * L, :]
         diag = dot_nt(form(own_form, z), jnp.concatenate([coupled] * 4, axis=0))
-        block = xf[z * ROWS : (z + 1) * ROWS, :]
+        diagonal = xf[z * ROWS : (z + 1) * ROWS, :]
         for s in range(4):
-            block = block + jnp.where(lane_group == s, diag[s * ROWS : (s + 1) * ROWS, :], 0.0)
-        re, im = block[:8], block[8:]
+            diagonal = diagonal + jnp.where(lane_group == s, diag[s * ROWS : (s + 1) * ROWS, :], 0.0)
+        re, im = diagonal[:8], diagonal[8:]
         arbuf[pl.ds(mine + z * ROWS, 8), :] = w_re * re - w_im * im
         arbuf[pl.ds(mine + z * ROWS + 8, 8), :] = w_re * im + w_im * re
 
@@ -340,7 +365,6 @@
 
 def body(t_mats, struct_table, zone_atoms, zone_size, pair_index, zone_link, weights, ne, na):
     adev = t_mats.shape[1]
-    slots = NB * NB
     given = (t_mats, struct_table, zone_atoms, zone_size, pair_index, zone_link, weights)
     bf16, f32 = jnp.bfloat16, jnp.float32
     green = pl.pallas_call(
@@ -350,7 +374,13 @@
         out_specs=pl.BlockSpec(memory_space=pltpu.VMEM),
         scratch_shapes=[
             *[pltpu.VMEM(a.shape, a.dtype) for a in given[:2]],
-            *[pltpu.SMEM(a.shape, a.dtype) for a in given[2:]],
+            pltpu.SMEM(zone_size.shape, zone_size.dtype),
+            pltpu.SMEM(weights.shape, weights.dtype),
+            *[pltpu.SMEM((Z * NB,), jnp.int32)] * (2 * adev),
+            *[pltpu.SMEM((Z,), jnp.int32)] * adev,
+            pltpu.SMEM((adev * NB * (NB + 1),), jnp.int32),
+            pltpu.SMEM((adev * NB * (NB + 1),), jnp.int32),
+            pltpu.SMEM((adev * NB * (NB + 1),), f32),
             pltpu.VMEM((adev * ROWS, LANES), f32),
             pltpu.VMEM((na, adev, ROWS, LANES), bf16),
             pltpu.VMEM((KTAB * ROWS, LANES), f32),
@@ -358,14 +388,16 @@
             pltpu.VMEM((adev, FORM, LANES), bf16),
             pltpu.VMEM((na * adev + 1, FORM, LANES), bf16),
             pltpu.VMEM((adev, KTAB + 1, L, FORM), f32),
-            pltpu.VMEM((adev * slots * L, LANES), bf16),
-            pltpu.VMEM((adev * NB * L, NB * LANES), bf16),
-            pltpu.VMEM((adev * L, NB * LANES), bf16),
-            pltpu.VMEM((adev * NB * L, LANES), bf16),
+            pltpu.VMEM((4 * adev * L, 4 * FORM), bf16),
+            pltpu.VMEM((adev * NB * NB * L, 4 * FORM), bf16),
+            pltpu.VMEM((adev * NB * L, NB * FORM), bf16),
+            pltpu.VMEM((adev * NB * L, 4 * FORM), bf16),
+            pltpu.VMEM((adev * L, NB * FORM), bf16),
+            pltpu.VMEM((adev * L, LANES), bf16),
             pltpu.VMEM((ne * adev * ROWS, LANES), f32),
-            pltpu.SemaphoreType.DMA((len(given),)),
+            pltpu.SemaphoreType.DMA((4 + 3 * adev,)),
             pltpu.SemaphoreType.DMA,
-            pltpu.SemaphoreType.DMA((4,)),
+            pltpu.SemaphoreType.DMA((8,)),
             pltpu.SemaphoreType.DMA,
             pltpu.SemaphoreType.DMA,
         ],

time: 22.9 us -> 22.8 us (level)
  Pallas kernels: 22.1 us -> 21.8 us
    pallas_call x1, Pallas kernels: 22.1 us -> 21.8 us  [body(): pl.pallas_call(functools.partial(kernel, ne, na, adev), out_shape=jax.Sha...]
where the time goes in v4:
time: 22.8 us; the launch traced here: 22.4 us
  Pallas kernels  21.8 us (96%)
  local copies, waits for them, and re-layouts  0.62 us (3%)
    pallas_call x1, Pallas kernels, body(): pl.pallas_call(functools.partial(kernel, ne, na, adev), out_shape=jax.Sha...  21.8 us
    reshape x1, local copies, waits for them, and re-layouts, body(): return green.reshape(adev, 2 * L * L)  0.62 us

profile of v4, /device:TPU:1, one launch (start us, length us, event | category | flops | bytes accessed | tf_op | source)
XLA Modules:
  0.0 22.4 jit_solution(6261393756954574830)
XLA Ops:
  0.0 21.8 %shard_map.73 = f32[32,128]{1,0:T(8,128)S(1)} custom-call(bf16[1,2,2048]{2,1,0:T(2,128)(2,1)} %t_hbm.1, bf16[1,64,2048]{2,1,0:T(8,128)(2,1)} %tab_hbm.1, s32[2,64]{1,0:T(2,128)} %atoms_hbm.1, s32[2]{0:T(128)} %size_hbm.1, s32[2,384]{1,0:T(2,128)} %pair_hbm.1, s32[2,384]{1,0:T(2,128)} %link_hbm.1, f32[1,2]{1,0:T(1,128)} %w_hbm.1), custom_call_target="tpu_custom_call" | custom-call | tf_op jit(solution)/shard_map/pallas_call | solution.py:370
  21.8 0.6 %reshape.3 = f32[2,2048]{1,0:T(2,128)} reshape(f32[32,128]{1,0:T(8,128)S(1)} %shard_map.73) | data formatting | bytes 32768 | tf_op jit(solution)/shard_map/reshape | solution.py:408
